TPU v7x, 256 devices: a whole 4x4x8 slice. The times are simulated.
256 devices in a mesh: dp: 16 (over z, y_hi), mp: 16 (over y_lo, x, core).
Axes of the slice: x: 4, y: 4 (y_hi: 2, y_lo: 2; y = y_hi * 2 + y_lo), z: 8, core: 2. Of those that a mesh axis runs over, the one named last changes fastest.
Arguments:
- activations: bfloat16 [2048, 4096], P('dp', 'mp'), may hold values from -6 to 6
- out_grad: bfloat16 [2048, 16384], P('dp', 'mp'), may hold values from -0.125 to 0.125
- block_slot: int32 [16, 16], replicated, may hold values from 0 to 15, each once within a row
- refresh_list: int32 [16, 4], replicated, may hold values from 0 to 15, as said below
- left_factor: float32 [16, 16, 512, 512], P('dp', 'mp'), as said below
- right_factor: float32 [16, 16, 512, 512], P('dp', 'mp'), as said below
- left_root: bfloat16 [16, 16, 512, 512], P('dp', 'mp'), as said below
- right_root: bfloat16 [16, 16, 512, 512], P('dp', 'mp'), as said below
Outputs:
- direction: bfloat16 [4096, 16384], P(None, 'mp')
- new_left_root: bfloat16 [16, 16, 512, 512], P('dp', 'mp')
- new_right_root: bfloat16 [16, 16, 512, 512], P('dp', 'mp')
Inputs may be any that keep to these rules, and one draw needn't show every extreme that they name: `block_slot`: each row is a permutation of the 16 slots; slot s of a strip belongs to dp index s. `refresh_list`: each row names 4 different blocks of its strip. `left_factor`: every tile is symmetric, with a positive diagonal that exceeds the sum of the magnitudes of its row's other entries. `right_factor`: every tile is symmetric, with a positive diagonal that exceeds the sum of the magnitudes of its row's other entries. `left_root`: every tile is symmetric. `right_root`: every tile is symmetric.
All inputs are finite; a program needn't handle non-finite values.
Results may differ from a plain program's by a relative error of at most 0.0064.
Values may be sent and summed in bfloat16 or wider, within the bound.
A program may use at most 128 MiB of HBM per device.

v0:
```python
import jax
import jax.numpy as jnp
from jax import lax
from jax.sharding import PartitionSpec as P

ITERS = 3


def inverse_root(statistic):
    size = statistic.shape[-1]
    identity = jnp.eye(size, dtype=jnp.float32)
    high = lax.Precision.HIGHEST
    scaling = 2.5 / jnp.sqrt(jnp.sum(statistic * statistic))
    iterate = identity * scaling**0.25
    powered = statistic * scaling
    for step in range(ITERS):
        factor = (5.0 * identity - powered) * 0.25
        iterate = jnp.dot(iterate, factor, precision=high)
        square = jnp.dot(factor, factor, precision=high)
        fourth = jnp.dot(square, square, precision=high)
        powered = jnp.dot(fourth, powered, precision=high)
    return iterate.astype(jnp.bfloat16)


def refresh_roots(statistics, previous, refreshed):

    def one_slot(items):
        statistic, earlier, flagged = items
        return lax.cond(flagged, lambda: inverse_root(statistic), lambda: earlier)

    return lax.map(one_slot, (statistics, previous, refreshed))


def body(
    activations,
    out_grad,
    block_slot,
    refresh_list,
    left_factor,
    right_factor,
    left_root,
    right_root,
):
    owner_index = lax.axis_index("dp")
    strip_index = lax.axis_index("mp")
    slots_here = left_factor.shape[0]
    width = left_factor.shape[-1]
    tok_rows = out_grad.shape[0]
    strip_cols = out_grad.shape[1]
    col_blocks = strip_cols // width
    full_act = lax.all_gather(activations, "mp", axis=1, tiled=True)
    row_blocks = full_act.shape[1] // width
    total_blocks = row_blocks * col_blocks
    slot_row = lax.dynamic_index_in_dim(block_slot, strip_index, 0, keepdims=False)
    pick_row = lax.dynamic_index_in_dim(refresh_list, strip_index, 0, keepdims=False)
    block_ids = jnp.arange(total_blocks, dtype=jnp.int32)
    slot_block = jnp.sum(
        jnp.where(slot_row[None, :] == block_ids[:, None], block_ids[None, :], 0), axis=1
    )
    owned_blocks = lax.dynamic_slice_in_dim(slot_block, owner_index * slots_here, slots_here)
    my_flags = jnp.any(pick_row[None, :] == owned_blocks[:, None], axis=1)
    act_blocks = full_act.reshape(tok_rows, row_blocks, width)
    cot_blocks = out_grad.reshape(tok_rows, col_blocks, width)
    left_part = jnp.take(act_blocks, slot_block // col_blocks, axis=1)
    right_part = jnp.take(cot_blocks, slot_block % col_blocks, axis=1)
    summed = lax.psum_scatter(
        jnp.einsum("tna,tnc->nac", left_part, right_part, preferred_element_type=jnp.float32),
        "dp",
        scatter_dimension=0,
        tiled=True,
    )
    gradient = summed.astype(jnp.bfloat16)
    left_stat = 0.9 * left_factor[:, 0] + jnp.einsum(
        "nab,ncb->nac", gradient, gradient, preferred_element_type=jnp.float32
    )
    right_stat = 0.9 * right_factor[:, 0] + jnp.einsum(
        "nba,nbc->nac", gradient, gradient, preferred_element_type=jnp.float32
    )
    previous_right = right_root[:, 0]
    new_left = refresh_roots(left_stat, left_root[:, 0], my_flags)
    new_right = refresh_roots(right_stat, previous_right, my_flags)
    mixed = jnp.einsum(
        "nab,nbc->nac", new_left, gradient, preferred_element_type=jnp.float32
    ).astype(jnp.bfloat16)
    precond = jnp.einsum("nab,nbc->nac", mixed, new_right, preferred_element_type=jnp.float32)
    grad_sq = jnp.sum(jnp.square(gradient.astype(jnp.float32)), axis=(1, 2))
    pre_sq = jnp.sum(precond * precond, axis=(1, 2))
    ratio = jnp.sqrt((grad_sq + 1e-06) / (pre_sq + 1e-06))
    tiles_out = (precond * ratio[:, None, None]).astype(jnp.bfloat16)
    every_slot = lax.all_gather(tiles_out, "dp", axis=0, tiled=True)
    by_block = jnp.take(every_slot, slot_row, axis=0)
    direction = (
        by_block.reshape(row_blocks, col_blocks, width, width)
        .transpose(0, 2, 1, 3)
        .reshape(row_blocks * width, strip_cols)
    )
    return (direction, new_left[:, None], new_right[:, None])


def solution(mesh):
    in_specs = (
        P("dp", "mp"),
        P("dp", "mp"),
        P(),
        P(),
        P("dp", "mp", None, None),
        P("dp", "mp", None, None),
        P("dp", "mp", None, None),
        P("dp", "mp", None, None),
    )
    out_specs = (P(None, "mp"), P("dp", "mp", None, None), P("dp", "mp", None, None))
    return jax.shard_map(body, mesh=mesh, in_specs=in_specs, out_specs=out_specs, check_vma=False)
```

profile of v0, /device:TPU:10, one launch (start us, length us, event | category | flops | bytes accessed | tf_op | source)
XLA Modules:
  0.0 588.0 jit_solution(10591519594889143535)
XLA Ops:
  7.2 0.0 copy-start.8
  7.2 0.0 copy-start.7
  7.2 0.0 all-gather.4.cloned.1.call-start
  7.2 1.9 copy.46
  9.1 1.9 copy.47
  11.0 0.0 copy-done.8
  11.0 0.7 copy.25
  11.8 0.0 all-gather.4.cloned.1.call-update
  11.8 0.0 reduce-scatter.2.cloned.1.call-start
  11.8 0.0 copy-done.7
  11.8 0.2 copy.27
  12.0 0.1 copy.28
  12.2 0.7 fusion.106
  12.9 0.1 select_reduce_fusion
  13.0 0.7 gather_fusion.1
  13.7 35.0 %all-gather.4.cloned.1.call-done = bf16[128,4096]{0,1:T(8,128)(2,1)} async-done(((bf16[128,256]{0,1:T(8,128)(2,1)}), bf16[128,4096]{0,1:T(8,128)(2,1)}) %all-gather.4.cloned.1.call-update) | async-done | bytes 1048592 | tf_op jit(solution)/shard_map/all_gather | solution.py:51
  48.8 1.5 copy.26
  50.3 2.0 gather_fusion
  52.3 9.8 %fusion.86 = f32[16,512,512]{2,1,0:T(8,128)} fusion(bf16[16,128,512]{2,1,0:T(8,128)(2,1)S(1)} %gather_fusion.1, bf16[16,128,512]{2,1,0:T(8,128)(2,1)} %gather_fusion, pred[16]{0:T(512)(128)(4,1)S(1)} %get-tuple-element.94, pred[16]{0:T(512)(128)(4,1)S(1)} %get-tuple-element.93), kind=kOutput, calls=%fused_computation.96 | convolution fusion | flops 1075838976 | bytes 20971552 | tf_op jit(solution)/shard_map/tna,tnc->nac/dot_general | solution.py:67
  62.1 0.0 copy-start.9
  62.1 0.0 reduce-scatter.2.cloned.1.call-update
  62.1 0.0 all-gather.6.cloned.1.call-start
  62.1 0.6 dynamic_slice.28
  62.7 0.0 copy-done.9
  62.8 1.3 fusion.101
  64.8 283.3 %reduce-scatter.2.cloned.1.call-done = f32[1,512,512]{2,1,0:T(8,128)} async-done(((f32[16,512,512]{2,1,0:T(8,128)}), f32[1,512,512]{2,1,0:T(8,128)}) %reduce-scatter.2.cloned.1.call-update) | async-done | bytes 1048592 | tf_op jit(solution)/shard_map/reduce_scatter | solution.py:66
  348.0 2.2 multiply_reduce_fusion.3
  350.2 0.0 copy-start.4
  350.2 0.5 fusion.99
  350.6 1.4 fusion.95
  352.1 0.1 broadcast.242
  352.2 0.0 copy-done.4
  352.2 9.7 %conditional.2 = (bf16[512,512]{1,0:T(8,128)(2,1)}, bf16[1,1,512,512]{3,2,1,0:T(8,128)(2,1)S(1)}) conditional(s32[]{:T(128)} %convert_element_type.30, (bf16[1,1,512,512]{3,2,1,0:T(8,128)(2,1)}) %tuple.55, (f32[1,1,512,512]{3,2,1,0:T(8,128)S(1)}, f32[512,512]{1,0:T(8,128)S(1)}, f32[512,512]{1,0:T(8,128)S(1)}) %tuple.63), branch_computations={%region_3.4_spmd, %region_4.6_spmd} | conditional | flops 14503378944 | bytes 36175996 | solution.py:29
  352.2 1.0 copy.39
  361.9 0.0 copy-start.5
  361.9 0.8 copy-done.5
  362.7 6.4 %conditional.3 = (bf16[512,512]{1,0:T(8,128)(2,1)}, bf16[1,1,512,512]{3,2,1,0:T(8,128)(2,1)S(1)}) conditional(s32[]{:T(128)} %convert_element_type.30, (bf16[1,1,512,512]{3,2,1,0:T(8,128)(2,1)}) %tuple.56, (f32[1,1,512,512]{3,2,1,0:T(8,128)}, f32[512,512]{1,0:T(8,128)S(1)}, f32[512,512]{1,0:T(8,128)}) %tuple.39), branch_computations={%region_6.7_spmd, %region_7.9_spmd} | conditional | flops 14503378944 | bytes 36175996 | solution.py:29
  362.7 1.0 copy.35
  369.1 0.0 copy-start.6
  369.1 0.8 copy-done.6
  369.9 2.7 multiply_reduce_fusion.2
  373.9 0.9 multiply_convert_fusion
  374.8 0.0 all-gather.6.cloned.1.call-update
  374.8 0.1 squeeze.39
  374.9 0.7 fusion.104
  375.6 170.0 %all-gather.6.cloned.1.call-done = bf16[8192,512]{1,0:T(8,128)(2,1)} async-done(((bf16[512,512]{1,0:T(8,128)(2,1)}), bf16[8192,512]{1,0:T(8,128)(2,1)}) %all-gather.6.cloned.1.call-update) | async-done | bytes 8388624 | tf_op jit(solution)/shard_map/all_gather | solution.py:90
  545.6 8.3 %gather_fusion.2 = bf16[16,512,512]{2,1,0:T(8,128)(2,1)} fusion(bf16[16,512,512]{2,1,0:T(8,128)(2,1)} %bitcast.90, s32[1024]{0:T(1024)S(1)} %pad_clamp_fusion), kind=kCustom, calls=%fused_computation.2 | custom fusion | bytes 16777280 | tf_op jit(solution)/shard_map/jit(_take)/gather | solution.py:91
  553.9 17.6 %broadcast_select_fusion = bf16[8,2,512,512]{3,1,2,0:T(2,128)(2,1)} fusion(pred[8,2]{1,0:T(8,128)(4,1)S(1)} %compare_and_fusion, bf16[8,2,512,512]{3,2,1,0:T(8,128)(2,1)} %bitcast.88), kind=kLoop, calls=%fused_computation.95 | loop fusion | flops 4194304 | bytes 16777232 | tf_op jit(solution)/shard_map/jit(_take)/select_n | solution.py:91
  571.5 9.5 %copy.32 = bf16[512,8,2,512]{3,1,2,0:T(8,128)(2,1)} copy(bf16[512,8,2,512]{3,2,1,0:T(2,128)(2,1)} %bitcast.89) | data formatting | bytes 16777216
  (5 shorter events, 0.1 us)
Async XLA Ops:
  7.2 3.9 copy-start.8
  7.2 4.7 copy-start.7
  7.2 41.6 %all-gather.4.cloned.1.call-start = ((), (), s32[]{:S(2)}) async-start(), calls=%async_computation.1 | async-start | bytes 1114112 | tf_op jit(solution)/shard_map/all_gather | solution.py:51
  11.8 336.2 %reduce-scatter.2.cloned.1.call-start = ((), (), s32[]{:S(2)}) async-start(), calls=%async_computation.2 | async-start | bytes 17825792 | tf_op jit(solution)/shard_map/reduce_scatter | solution.py:66
  62.1 0.7 copy-start.9
  62.1 483.5 %all-gather.6.cloned.1.call-start = ((), (), s32[]{:S(2)}) async-start(), calls=%async_computation.3 | async-start | bytes 8912896 | tf_op jit(solution)/shard_map/all_gather | solution.py:90
  350.2 2.0 copy-start.4
  361.9 0.8 copy-start.5
  369.1 0.8 copy-start.6
Sparse Core Ops, SparseCore 0:
  11.9 36.8 all-gather.3
  62.2 285.7 reduce-scatter.1
  375.0 170.5 all-gather.5
where the time goes:
time: 594 us; the launch traced here: 588 us
  waiting for transfers between devices  488 us (82%)
  local copies, waits for them, and re-layouts  32 us (5%)
  other arithmetic  22.9 us (4%)
  between operations  16.4 us (3%)
  matrix products  14.3 us (2%)
  loops' own time  14 us (2%)
    reduce_scatter x1, waiting for transfers between devices, body(): lax.psum_scatter(jnp.einsum('tna,tnc->nac', left_part, right_part, prefer...  283 us
    all_gather x1, waiting for transfers between devices, body(): every_slot = lax.all_gather(tiles_out, 'dp', axis=0, tiled=True)  170 us
    all_gather x1, waiting for transfers between devices, body(): full_act = lax.all_gather(activations, 'mp', axis=1, tiled=True)  35 us
    select_n x2, other arithmetic, body(): by_block = jnp.take(every_slot, slot_row, axis=0)  18.3 us
    unnamed x17, local copies, waits for them, and re-layouts  15.8 us
    another operation x2, loops' own time, one_slot(): return lax.cond(flagged, lambda: inverse_root(statistic), lambda: earlier)  14 us
  transfers between devices with their start and end apart: 3, of which 3 were waited for; matrix products, arithmetic and copies ran while one was open for 1% of the time, Pallas kernels for 0%

commit v1 on v0

v1 whole, which is shorter than its diff:
```python
import functools

import jax
import jax.numpy as jnp
from jax import lax
from jax.experimental import pallas as pl
from jax.experimental.pallas import tpu as pltpu
from jax.sharding import PartitionSpec as P

NZ, NX, NY = 8, 4, 4
SIDE = 512
FEAT = 64
A_ROWS = 288
HALF = A_ROWS // 2
MESH = pl.DeviceIdType.MESH
VMEM_LIMIT = 48 * 1024 * 1024


def place():
    dp, mp = lax.axis_index("dp"), lax.axis_index("mp")
    return dp // 2, dp % 2, mp // 8, (mp // 2) % 4, mp % 2


def device(z, h, l, x, k):
    return (2 * z + h, 8 * l + 2 * x + k)


def gradient_kernel(
    slots_ref, act_ref, out_ref, grad_ref,
    cot, act, flipped, total, pieces, outgoing, tile,
    swap_s, swap_r, ring_s, ring_r, turn_s, turn_r, plane_s, plane_r,
    pass_s, pass_r, give_s, give_r, local_s,
):
    z, h, l, x, k = place()
    dp, mp = lax.axis_index("dp"), lax.axis_index("mp")
    y = 2 * h + l
    r = 4 * l + x
    up, down = (z + 1) % NZ, (z + NZ - 1) % NZ

    barrier = pltpu.get_barrier_semaphore()

    def greet(target):
        pl.semaphore_signal(barrier, inc=1, device_id=target, device_id_type=MESH)

    for step in range(1, 16):
        greet(((dp + step) % 16, mp))
    for dy in range(NY):
        for dx in range(NX):
            if (dy, dx) != (0, 0):
                ty, tx = (y + dy) % NY, (x + dx) % NX
                greet(device(z, ty // 2, ty % 2, tx, k))
    for step in range(NZ):
        greet(device((z + step) % NZ, h, l, x, 1 - k))

    for c in range(2):
        cot[z, pl.ds(h * 128, 128), c * 256 : c * 256 + 256] = out_ref[
            :, pl.ds(pl.multiple_of(c * 512 + 256 * h, 256), 256)
        ]
    flipped[...] = act_ref[...].astype(jnp.float32).T.astype(jnp.bfloat16)
    pl.semaphore_wait(barrier, 38)

    def send(src, dst, ssem, rsem, target):
        copy = pltpu.make_async_remote_copy(
            src_ref=src, dst_ref=dst, send_sem=ssem, recv_sem=rsem, device_id=target, device_id_type=MESH
        )
        copy.start()
        return copy

    pending = []

    def turn_view(source):
        return act.at[source // 2, source % 2, r, :, pl.ds(pl.multiple_of(h * 128, 128), 128)]

    for j in range(4):
        target = 4 * k + j
        here = jnp.logical_and(target == z, z % 2 == k)
        src = flipped.at[j * FEAT : (j + 1) * FEAT, :]

        @pl.when(jnp.logical_not(here))
        def _():
            send(src, turn_view(z), turn_s.at[j], turn_r.at[z], device(target, h, l, x, z % 2))

        @pl.when(here)
        def _():
            pltpu.make_async_copy(src, turn_view(z), turn_r.at[z]).start()

    for c in range(2):
        pending.append(
            send(
                out_ref.at[:, pl.ds(pl.multiple_of(c * 512 + 256 * (1 - h), 256), 256)],
                cot.at[z, pl.ds(pl.multiple_of(h * 128, 128), 128), pl.ds(c * 256, 256)],
                swap_s.at[c], swap_r.at[c], (2 * z + 1 - h, mp),
            )
        )

    def unit(source, u):
        return cot.at[source, pl.ds(pl.multiple_of(u * 128, 128), 128), :]

    def ring(direction, step, u):
        source = (z + NZ - step) % NZ if direction == 0 else (z + step) % NZ
        target = up if direction == 0 else down
        view = unit(source, u)
        pending.append(
            send(view, view, ring_s.at[direction, step, u], ring_r.at[direction, step, u], (2 * target + h, mp))
        )

    def ring_wait(direction, step, u):
        source = (z + NZ - step) % NZ if direction == 0 else (z + step) % NZ
        view = unit(source, u)
        pltpu.make_async_remote_copy(
            src_ref=view, dst_ref=view, send_sem=ring_s.at[direction, step - 1, u],
            recv_sem=ring_r.at[direction, step - 1, u], device_id=(dp, mp), device_id_type=MESH,
        ).wait_recv()

    ring(0, 0, h)
    ring(1, 0, h)

    for i in range(4):
        source = 2 * i + k
        view = turn_view(source)
        pltpu.make_async_copy(view, view, turn_r.at[source]).wait()

    def plane_view(row, half):
        return act.at[:, k, row, :, pl.ds(pl.multiple_of(half * 128, 128), 128)]

    for dy in range(NY):
        for dx in range(NX):
            if (dy, dx) != (0, 0):
                ty, tx = (y + dy) % NY, (x + dx) % NX
                view = plane_view(r, h)
                pending.append(
                    send(view, view, plane_s.at[4 * dy + dx], plane_r.at[4 * dy + dx], device(z, ty // 2, ty % 2, tx, k))
                )

    for c in range(2):
        view = cot.at[z, pl.ds(pl.multiple_of((1 - h) * 128, 128), 128), pl.ds(c * 256, 256)]
        pltpu.make_async_copy(view, view, swap_r.at[c]).wait()
    ring(0, 0, 1 - h)
    ring(1, 0, 1 - h)

    for step in (1, 2):
        for u in (h, 1 - h):
            for direction in (0, 1):
                ring_wait(direction, step, u)
                ring(direction, step, u)

    for dy in range(NY):
        for dx in range(NX):
            if (dy, dx) != (0, 0):
                sy, sx = (y + NY - dy) % NY, (x + NX - dx) % NX
                view = plane_view(4 * (sy % 2) + sx, sy // 2)
                pltpu.make_async_copy(view, view, plane_r.at[4 * dy + dx]).wait()
    for row in range(8):
        view = act.at[:, k, row]
        pending.append(send(view, view, pass_s.at[row], pass_r.at[row], device(z, h, l, x, 1 - k)))

    for u in (h, 1 - h):
        for direction in (0, 1):
            ring_wait(direction, 3, u)
    ring(0, 3, 0)
    ring(1, 3, 1)

    for row in range(8):
        view = act.at[:, 1 - k, row]
        pltpu.make_async_copy(view, view, pass_r.at[row]).wait()

    def product(source):
        return jnp.dot(
            act[source // 2, source % 2].reshape(8 * FEAT, 256), cot[source], preferred_element_type=jnp.float32
        )

    total[...] = product(z)

    @pl.loop(1, 4)
    def _(step):
        total[...] += product((z + step) % NZ)
        total[...] += product((z + NZ - step) % NZ)

    ring_wait(0, 4, 0)
    ring_wait(1, 4, 1)
    total[...] += product((z + 4) % NZ)

    for row in range(8):
        for c in range(2):
            pieces[2 * row + c] = total[row * FEAT : (row + 1) * FEAT, c * 256 : (c + 1) * 256].astype(jnp.bfloat16)

    def spot(slot):
        return tile.at[
            pl.ds(pl.multiple_of((slot // 2) * FEAT, FEAT), FEAT), pl.ds(pl.multiple_of((slot % 2) * 256, 256), 256)
        ]

    def held(slot):
        found = jnp.int32(0)
        for b in range(16):
            found = jnp.maximum(found, jnp.where(slots_ref[mp, b] == slot, b, 0))
        return found

    @pl.loop(1, 16)
    def _(step):
        slot = (dp + step) % 16
        outgoing[slot] = pieces[held(slot)]
        send(outgoing.at[slot], spot(dp), give_s.at[slot], give_r.at[dp], (slot, mp))

    outgoing[dp] = pieces[held(dp)]
    own = pltpu.make_async_copy(outgoing.at[dp], spot(dp), local_s)
    own.start()
    own.wait()

    @pl.loop(1, 16)
    def _(step):
        slot = (dp + step) % 16
        view = spot(slot)
        pltpu.make_async_copy(view, view, give_r.at[slot]).wait()
        pltpu.make_async_copy(outgoing.at[slot], outgoing.at[slot], give_s.at[slot]).wait()

    for copy in pending:
        copy.wait_send()
    for j in range(4):
        here = jnp.logical_and(4 * k + j == z, z % 2 == k)
        src = flipped.at[j * FEAT : (j + 1) * FEAT, :]

        @pl.when(jnp.logical_not(here))
        def _():
            pltpu.make_async_copy(src, src, turn_s.at[j]).wait()

    grad_ref[...] = tile[...]


def owned_gradient(block_slot, activations, out_grad):
    dma = pltpu.SemaphoreType.DMA
    vmem = pl.BlockSpec(memory_space=pltpu.VMEM)
    return pl.pallas_call(
        gradient_kernel,
        name="owned_gradient",
        out_shape=jax.ShapeDtypeStruct((SIDE, SIDE), jnp.bfloat16),
        in_specs=[pl.BlockSpec(memory_space=pltpu.SMEM), vmem, vmem],
        out_specs=vmem,
        scratch_shapes=[
            pltpu.VMEM((NZ, 256, SIDE), jnp.bfloat16),
            pltpu.VMEM((4, 2, 8, FEAT, 256), jnp.bfloat16),
            pltpu.VMEM((256, 128), jnp.bfloat16),
            pltpu.VMEM((8 * FEAT, SIDE), jnp.float32),
            pltpu.VMEM((16, FEAT, 256), jnp.bfloat16),
            pltpu.VMEM((16, FEAT, 256), jnp.bfloat16),
            pltpu.VMEM((SIDE, SIDE), jnp.bfloat16),
            dma((2,)), dma((2,)), dma((2, 4, 2)), dma((2, 4, 2)), dma((4,)), dma((NZ,)), dma((16,)), dma((16,)),
            dma((8,)), dma((8,)), dma((16,)), dma((16,)), dma,
        ],
        compiler_params=pltpu.CompilerParams(collective_id=1, has_side_effects=True, vmem_limit_bytes=VMEM_LIMIT),
        cost_estimate=pl.CostEstimate(flops=2 * 512 * 512 * 2048, bytes_accessed=1 << 20, transcendentals=0),
    )(block_slot, activations, out_grad)


def matmul(left, right):
    return jnp.dot(left.astype(jnp.bfloat16), right.astype(jnp.bfloat16), preferred_element_type=jnp.float32)


def inverse_root(statistic):
    rows = lax.broadcasted_iota(jnp.int32, statistic.shape, 0)
    cols = lax.broadcasted_iota(jnp.int32, statistic.shape, 1)
    identity = jnp.where(rows == cols, 1.0, 0.0).astype(jnp.float32)
    scaling = 2.5 / jnp.sqrt(jnp.sum(statistic * statistic))

    def power(powered):
        dev = 0.25 * powered
        square = 1.5625 * identity - 2.5 * dev + matmul(dev, dev)
        return dev, matmul(matmul(square, square), powered)

    first, powered = power(statistic * scaling)
    second, powered = power(powered)
    third = 0.25 * powered
    pair = 1.25 * (first + second) - matmul(first, second)
    result = 1.953125 * identity - 1.25 * pair - 1.5625 * third + matmul(pair, third)
    return (result * jnp.sqrt(jnp.sqrt(scaling))).astype(jnp.bfloat16)


def slot_kernel(
    slots_ref, refresh_ref, grad_ref, lf_ref, rf_ref, lr_ref, rr_ref, dir_ref, nl_ref, nr_ref
):
    dp, mp = lax.axis_index("dp"), lax.axis_index("mp")
    mine = jnp.int32(0)
    for b in range(16):
        mine += jnp.where(slots_ref[mp, b] == dp, b, 0)
    hits = jnp.int32(0)
    for j in range(4):
        hits += jnp.where(refresh_ref[mp, j] == mine, 1, 0)

    @pl.when(hits > 0)
    def _():
        grad = grad_ref[...]
        left = lax.dot_general(grad, grad, (((1,), (1,)), ((), ())), preferred_element_type=jnp.float32)
        nl_ref[...] = inverse_root(0.9 * lf_ref[...] + left)
        right = lax.dot_general(grad, grad, (((0,), (0,)), ((), ())), preferred_element_type=jnp.float32)
        nr_ref[...] = inverse_root(0.9 * rf_ref[...] + right)

    @pl.when(hits == 0)
    def _():
        nl_ref[...] = lr_ref[...]
        nr_ref[...] = rr_ref[...]

    grad = grad_ref[...]
    mixed = jnp.dot(nl_ref[...], grad, preferred_element_type=jnp.float32).astype(jnp.bfloat16)
    precond = jnp.dot(mixed, nr_ref[...], preferred_element_type=jnp.float32)
    wide = grad.astype(jnp.float32)
    ratio = jnp.sqrt((jnp.sum(wide * wide) + 1e-06) / (jnp.sum(precond * precond) + 1e-06))
    dir_ref[...] = (precond * ratio).astype(jnp.bfloat16)


def slot_step(block_slot, refresh_list, gradient, left_factor, right_factor, left_root, right_root):
    vmem = pl.BlockSpec(memory_space=pltpu.VMEM)
    smem = pl.BlockSpec(memory_space=pltpu.SMEM)
    tile = jax.ShapeDtypeStruct((SIDE, SIDE), jnp.bfloat16)
    return pl.pallas_call(
        slot_kernel,
        name="slot_step",
        out_shape=(tile, tile, tile),
        in_specs=[smem, smem] + [vmem] * 5,
        out_specs=(vmem, vmem, vmem),
        compiler_params=pltpu.CompilerParams(vmem_limit_bytes=VMEM_LIMIT),
        cost_estimate=pl.CostEstimate(flops=2 * 512**3 * 20, bytes_accessed=5 << 20, transcendentals=0),
    )(block_slot, refresh_list, gradient, left_factor, right_factor, left_root, right_root)


def spread_kernel(
    tile_ref, every, z_s, z_r, zb_s, zb_r, y_s, y_r, yb_s, yb_r, local_s
):
    z, h, l, x, k = place()
    dp, mp = lax.axis_index("dp"), lax.axis_index("mp")
    ends = ((2 * ((z + 1) % NZ) + h, mp), (2 * ((z + NZ - 1) % NZ) + h, mp))
    partner = (2 * z + 1 - h, mp)
    barrier = pltpu.get_barrier_semaphore()
    for target in (*ends, partner):
        pl.semaphore_signal(barrier, inc=1, device_id=target, device_id_type=MESH)
    own = pltpu.make_async_copy(tile_ref, every.at[dp], local_s)
    own.start()
    pl.semaphore_wait(barrier, 3)

    pending = []

    def send(src, dst, ssem, rsem, target):
        copy = pltpu.make_async_remote_copy(
            src_ref=src, dst_ref=dst, send_sem=ssem, recv_sem=rsem, device_id=target, device_id_type=MESH
        )
        copy.start()
        pending.append(copy)

    def arrived(view, sem):
        pltpu.make_async_copy(view, view, sem).wait()

    def source(direction, step):
        return (z + NZ - step) % NZ if direction == 0 else (z + step) % NZ

    def a_rows(direction, step):
        if step < 3:
            return pl.ds(0, A_ROWS)
        return pl.ds(direction * HALF, HALF)

    def a_view(slot, rows):
        return every.at[slot, rows, :]

    def b_view(slot):
        return every.at[slot, pl.ds(A_ROWS, SIDE - A_ROWS), :]

    def z_a(direction, step):
        rows = a_rows(direction, step)
        dst = a_view(2 * source(direction, step) + h, rows)
        src = tile_ref.at[rows, :] if step == 0 else dst
        send(src, dst, z_s.at[direction, step], z_r.at[direction, step], ends[direction])

    def z_b(direction, step, u):
        dst = b_view(2 * source(direction, step) + u)
        src = dst
        send(src, dst, zb_s.at[direction, step, u], zb_r.at[direction, step, u], ends[direction])

    def y_a(index, slot, rows, src=None):
        dst = a_view(slot, rows)
        send(dst if src is None else src, dst, y_s.at[index], y_r.at[index], partner)

    full = pl.ds(0, A_ROWS)
    z_a(0, 0)
    z_a(1, 0)
    send(tile_ref.at[pl.ds(A_ROWS, SIDE - A_ROWS), :], b_view(dp), yb_s, yb_r, partner)
    y_a(0, dp, full, tile_ref.at[full, :])
    own.wait()
    z_b(0, 0, h)
    z_b(1, 0, h)
    arrived(b_view(2 * z + 1 - h), yb_r)
    z_b(0, 0, 1 - h)
    z_b(1, 0, 1 - h)

    for step in (1, 2, 3):
        for direction in (0, 1):
            slot = 2 * source(direction, step) + h
            arrived(a_view(slot, full), z_r.at[direction, step - 1])
            z_a(direction, step)
            y_a(1 + 3 * direction + step - 1, slot, full)
        for u in (h, 1 - h):
            for direction in (0, 1):
                arrived(b_view(2 * source(direction, step) + u), zb_r.at[direction, step - 1, u])
                if step < 3:
                    z_b(direction, step, u)
        if step == 3:
            z_b(0, 3, 0)
            z_b(1, 3, 1)
    for direction in (0, 1):
        rows = a_rows(direction, 3)
        slot = 2 * source(direction, 4) + h
        arrived(a_view(slot, rows), z_r.at[direction, 3])
        y_a(7 + direction, slot, rows)
    arrived(b_view(2 * source(0, 4)), zb_r.at[0, 3, 0])
    arrived(b_view(2 * source(1, 4) + 1), zb_r.at[1, 3, 1])

    other = 1 - h
    arrived(a_view(2 * z + other, full), y_r.at[0])
    for direction in (0, 1):
        for step in (1, 2, 3):
            arrived(a_view(2 * source(direction, step) + other, full), y_r.at[1 + 3 * direction + step - 1])
    for direction in (0, 1):
        arrived(a_view(2 * source(direction, 4) + other, a_rows(direction, 3)), y_r.at[7 + direction])
    for copy in pending:
        copy.wait_send()


def spread(tile):
    dma = pltpu.SemaphoreType.DMA
    return pl.pallas_call(
        spread_kernel,
        name="spread",
        out_shape=jax.ShapeDtypeStruct((16, SIDE, SIDE), jnp.bfloat16),
        in_specs=[pl.BlockSpec(memory_space=pl.ANY)],
        out_specs=pl.BlockSpec(memory_space=pl.ANY),
        scratch_shapes=[
            dma((2, 4)), dma((2, 4)), dma((2, 4, 2)), dma((2, 4, 2)), dma((9,)), dma((9,)), dma, dma, dma,
        ],
        compiler_params=pltpu.CompilerParams(collective_id=2, has_side_effects=True),
        cost_estimate=pl.CostEstimate(flops=0, bytes_accessed=16 << 20, transcendentals=0),
    )(tile)


def arrange_kernel(slots_ref, every, out_ref):
    out_ref[...] = every[0]


def arrange(slot_row, every):
    return pl.pallas_call(
        arrange_kernel,
        name="arrange",
        grid_spec=pltpu.PrefetchScalarGridSpec(
            num_scalar_prefetch=1,
            grid=(16,),
            in_specs=[pl.BlockSpec((1, SIDE, SIDE), lambda b, slots: (slots[b], 0, 0))],
            out_specs=pl.BlockSpec((SIDE, SIDE), lambda b, slots: (b // 2, b % 2)),
        ),
        out_shape=jax.ShapeDtypeStruct((8 * SIDE, 2 * SIDE), jnp.bfloat16),
        cost_estimate=pl.CostEstimate(flops=0, bytes_accessed=16 << 20, transcendentals=0),
    )(slot_row, every)


def body(
    activations,
    out_grad,
    block_slot,
    refresh_list,
    left_factor,
    right_factor,
    left_root,
    right_root,
):
    slot_row = lax.dynamic_index_in_dim(block_slot, lax.axis_index("mp"), 0, keepdims=False)
    gradient = owned_gradient(block_slot, activations, out_grad)
    tile, new_left, new_right = slot_step(
        block_slot, refresh_list, gradient,
        left_factor[0, 0], right_factor[0, 0], left_root[0, 0], right_root[0, 0],
    )
    direction = arrange(slot_row, spread(tile))
    return (direction, new_left[None, None], new_right[None, None])


def solution(mesh):
    in_specs = (
        P("dp", "mp"),
        P("dp", "mp"),
        P(),
        P(),
        P("dp", "mp", None, None),
        P("dp", "mp", None, None),
        P("dp", "mp", None, None),
        P("dp", "mp", None, None),
    )
    out_specs = (P(None, "mp"), P("dp", "mp", None, None), P("dp", "mp", None, None))
    return jax.shard_map(body, mesh=mesh, in_specs=in_specs, out_specs=out_specs, check_vma=False)
```

time: 594 us -> 157 us (0.26)
  the two profiles are of different devices: /device:TPU:10 before, /device:TPU:14 now
where the time goes in v1:
time: 157 us; the launch traced here: 156 us
  Pallas kernels  146 us (93%)
  local copies, waits for them, and re-layouts  9.8 us (6%)
    pallas_call x1, Pallas kernels, spread(): pl.pallas_call(spread_kernel, name='spread', out_shape=jax.ShapeDtypeStru...  81.1 us
    pallas_call x1, Pallas kernels, owned_gradient(): pl.pallas_call(gradient_kernel, name='owned_gradient', out_shape=jax.Shap...  50.3 us
    pallas_call x1, Pallas kernels, arrange(): pl.pallas_call(arrange_kernel, name='arrange', grid_spec=pltpu.PrefetchSc...  12.6 us
    unnamed x17, local copies, waits for them, and re-layouts  8.56 us

profile of v1, /device:TPU:14, one launch (start us, length us, event | category | flops | bytes accessed | tf_op | source)
XLA Modules:
  0.0 156.5 jit_solution(16546350361798827573)
XLA Ops:
  0.6 1.2 dynamic-slice_bitcast_fusion.slots_ref
  1.9 0.8 copy.11.refresh_ref
  2.6 0.0 copy-start.5
  2.6 0.9 copy-done.5
  3.6 0.0 copy-start.6
  3.6 0.8 copy-done.6
  4.4 0.0 copy-start.7
  4.4 0.7 copy-done.7
  5.1 50.3 %owned_gradient.1.grad_ref = bf16[512,512]{1,0:T(8,128)(2,1)S(1)} custom-call(s32[16,16]{1,0:T(8,128)S(1)} %copy-done.7, bf16[128,256]{1,0:T(8,128)(2,1)S(1)} %copy-done.6, bf16[128,1024]{1,0:T(8,128)(2,1)S(1)} %copy-done.5), custom_call_target="tpu_custom_call" | custom-call | flops 1073741824 | bytes 1048576 | tf_op jit(solution)/shard_map/owned_gradient/pallas_call | solution.py:232
  55.4 0.0 copy-start.1
  55.4 1.2 copy-done.1
  56.6 0.0 copy-start.2
  56.6 1.2 copy-done.2
  57.9 0.0 copy-start.3
  57.9 1.0 copy-done.3
  58.9 0.0 copy-start.4
  58.9 1.0 copy-done.4
  60.0 2.1 %slot_step.1 = (bf16[512,512]{1,0:T(8,128)(2,1)S(1)}, bf16[512,512]{1,0:T(8,128)(2,1)}, bf16[512,512]{1,0:T(8,128)(2,1)}) custom-call(s32[16,16]{1,0:T(8,128)S(1)} %copy-done.7, s32[16,4]{1,0:T(8,128)S(1)} %copy.11.refresh_ref, bf16[512,512]{1,0:T(8,128)(2,1)S(1)} %owned_gradient.1.grad_ref, f32[512,512]{1,0:T(8,128)S(1)} %bitcast.8, ...), custom_call_target="tpu_custom_call" | custom-call | flops 5368709120 | bytes 5242880 | tf_op jit(solution)/shard_map/slot_step/pallas_call | solution.py:313
  62.0 0.0 copy-start
  62.0 0.8 copy-done
  62.8 81.1 %spread.1.every = bf16[16,512,512]{2,1,0:T(8,128)(2,1)} custom-call(bf16[512,512]{1,0:T(8,128)(2,1)} %copy-done), custom_call_target="tpu_custom_call" | custom-call | bytes 16777216 | tf_op jit(solution)/shard_map/spread/pallas_call | solution.py:426
  143.9 12.6 %arrange.1 = bf16[4096,1024]{1,0:T(8,128)(2,1)} custom-call(s32[16]{0:T(128)} %dynamic-slice_bitcast_fusion.slots_ref, bf16[16,512,512]{2,1,0:T(8,128)(2,1)} %spread.1.every), custom_call_target="tpu_custom_call" | custom-call | bytes 16777216 | tf_op jit(solution)/shard_map/arrange/pallas_call | solution.py:445
Async XLA Ops:
  2.6 0.9 copy-start.5
  3.6 0.8 copy-start.6
  4.4 0.7 copy-start.7
  55.4 1.2 copy-start.1
  56.6 1.2 copy-start.2
  57.9 1.0 copy-start.3
  58.9 1.0 copy-start.4
  62.0 0.8 copy-start

commit v2 on v1

--- a/solution.py
+++ b/solution.py
@@ -1,5 +1,3 @@
-import functools
-
 import jax
 import jax.numpy as jnp
 from jax import lax
@@ -13,7 +11,7 @@
 A_ROWS = 288
 HALF = A_ROWS // 2
 MESH = pl.DeviceIdType.MESH
-VMEM_LIMIT = 48 * 1024 * 1024
+VMEM_LIMIT = 40 * 1024 * 1024
 
 
 def place():
@@ -25,11 +23,35 @@
     return (2 * z + h, 8 * l + 2 * x + k)
 
 
-def gradient_kernel(
-    slots_ref, act_ref, out_ref, grad_ref,
-    cot, act, flipped, total, pieces, outgoing, tile,
+def matmul(left, right):
+    return jnp.dot(left.astype(jnp.bfloat16), right.astype(jnp.bfloat16), preferred_element_type=jnp.float32)
+
+
+def inverse_roots(statistics):
+    shape = statistics[0].shape
+    rows = lax.broadcasted_iota(jnp.int32, shape, 0)
+    cols = lax.broadcasted_iota(jnp.int32, shape, 1)
+    identity = jnp.where(rows == cols, 1.0, 0.0).astype(jnp.float32)
+    scaling = [2.5 / jnp.sqrt(jnp.sum(a * a)) for a in statistics]
+    powered = [a * c for a, c in zip(statistics, scaling)]
+    parts = []
+    for _ in range(2):
+        dev = [0.25 * m for m in powered]
+        parts.append(dev)
+        square = [1.5625 * identity - 2.5 * e + matmul(e, e) for e in dev]
+        fourth = [matmul(f, f) for f in square]
+        powered = [matmul(f, m) for f, m in zip(fourth, powered)]
+    third = [0.25 * m for m in powered]
+    pair = [1.25 * (e + f) - matmul(e, f) for e, f in zip(*parts)]
+    result = [1.953125 * identity - 1.25 * p - 1.5625 * e + matmul(p, e) for p, e in zip(pair, third)]
+    return [(x * jnp.sqrt(jnp.sqrt(c))).astype(jnp.bfloat16) for x, c in zip(result, scaling)]
+
+
+def step_kernel(
+    slots_hbm, refresh_hbm, act_hbm, out_hbm, lf_hbm, rf_hbm, lr_hbm, rr_hbm, every, nl_ref, nr_ref,
+    slots_ref, refresh_ref, act_ref, out_ref, lf_ref, rf_ref, lr_ref, rr_ref, load_s, cot, act, flipped, total, pieces, outgoing, tile,
     swap_s, swap_r, ring_s, ring_r, turn_s, turn_r, plane_s, plane_r,
-    pass_s, pass_r, give_s, give_r, local_s,
+    pass_s, pass_r, give_s, give_r, local_s, z_s, z_r, zb_s, zb_r, y_s, y_r, yb_s, yb_r,
 ):
     z, h, l, x, k = place()
     dp, mp = lax.axis_index("dp"), lax.axis_index("mp")
@@ -37,6 +59,17 @@
     r = 4 * l + x
     up, down = (z + 1) % NZ, (z + NZ - 1) % NZ
 
+    loads = [
+        pltpu.make_async_copy(src, dst, load_s.at[i])
+        for i, (src, dst) in enumerate(
+            (
+                (act_hbm, act_ref), (out_hbm, out_ref), (slots_hbm, slots_ref), (refresh_hbm, refresh_ref),
+                (lf_hbm, lf_ref), (rf_hbm, rf_ref), (lr_hbm, lr_ref), (rr_hbm, rr_ref),
+            )
+        )
+    ]
+    for copy in loads:
+        copy.start()
     barrier = pltpu.get_barrier_semaphore()
 
     def greet(target):
@@ -52,6 +85,8 @@
     for step in range(NZ):
         greet(device((z + step) % NZ, h, l, x, 1 - k))
 
+    for copy in loads[:4]:
+        copy.wait()
     for c in range(2):
         cot[z, pl.ds(h * 128, 128), c * 256 : c * 256 + 256] = out_ref[
             :, pl.ds(pl.multiple_of(c * 512 + 256 * h, 256), 256)
@@ -213,136 +248,27 @@
         pltpu.make_async_copy(view, view, give_r.at[slot]).wait()
         pltpu.make_async_copy(outgoing.at[slot], outgoing.at[slot], give_s.at[slot]).wait()
 
-    for copy in pending:
-        copy.wait_send()
-    for j in range(4):
-        here = jnp.logical_and(4 * k + j == z, z % 2 == k)
-        src = flipped.at[j * FEAT : (j + 1) * FEAT, :]
-
-        @pl.when(jnp.logical_not(here))
-        def _():
-            pltpu.make_async_copy(src, src, turn_s.at[j]).wait()
-
-    grad_ref[...] = tile[...]
-
-
-def owned_gradient(block_slot, activations, out_grad):
-    dma = pltpu.SemaphoreType.DMA
-    vmem = pl.BlockSpec(memory_space=pltpu.VMEM)
-    return pl.pallas_call(
-        gradient_kernel,
-        name="owned_gradient",
-        out_shape=jax.ShapeDtypeStruct((SIDE, SIDE), jnp.bfloat16),
-        in_specs=[pl.BlockSpec(memory_space=pltpu.SMEM), vmem, vmem],
-        out_specs=vmem,
-        scratch_shapes=[
-            pltpu.VMEM((NZ, 256, SIDE), jnp.bfloat16),
-            pltpu.VMEM((4, 2, 8, FEAT, 256), jnp.bfloat16),
-            pltpu.VMEM((256, 128), jnp.bfloat16),
-            pltpu.VMEM((8 * FEAT, SIDE), jnp.float32),
-            pltpu.VMEM((16, FEAT, 256), jnp.bfloat16),
-            pltpu.VMEM((16, FEAT, 256), jnp.bfloat16),
-            pltpu.VMEM((SIDE, SIDE), jnp.bfloat16),
-            dma((2,)), dma((2,)), dma((2, 4, 2)), dma((2, 4, 2)), dma((4,)), dma((NZ,)), dma((16,)), dma((16,)),
-            dma((8,)), dma((8,)), dma((16,)), dma((16,)), dma,
-        ],
-        compiler_params=pltpu.CompilerParams(collective_id=1, has_side_effects=True, vmem_limit_bytes=VMEM_LIMIT),
-        cost_estimate=pl.CostEstimate(flops=2 * 512 * 512 * 2048, bytes_accessed=1 << 20, transcendentals=0),
-    )(block_slot, activations, out_grad)
-
-
-def matmul(left, right):
-    return jnp.dot(left.astype(jnp.bfloat16), right.astype(jnp.bfloat16), preferred_element_type=jnp.float32)
-
-
-def inverse_root(statistic):
-    rows = lax.broadcasted_iota(jnp.int32, statistic.shape, 0)
-    cols = lax.broadcasted_iota(jnp.int32, statistic.shape, 1)
-    identity = jnp.where(rows == cols, 1.0, 0.0).astype(jnp.float32)
-    scaling = 2.5 / jnp.sqrt(jnp.sum(statistic * statistic))
-
-    def power(powered):
-        dev = 0.25 * powered
-        square = 1.5625 * identity - 2.5 * dev + matmul(dev, dev)
-        return dev, matmul(matmul(square, square), powered)
-
-    first, powered = power(statistic * scaling)
-    second, powered = power(powered)
-    third = 0.25 * powered
-    pair = 1.25 * (first + second) - matmul(first, second)
-    result = 1.953125 * identity - 1.25 * pair - 1.5625 * third + matmul(pair, third)
-    return (result * jnp.sqrt(jnp.sqrt(scaling))).astype(jnp.bfloat16)
-
-
-def slot_kernel(
-    slots_ref, refresh_ref, grad_ref, lf_ref, rf_ref, lr_ref, rr_ref, dir_ref, nl_ref, nr_ref
-):
-    dp, mp = lax.axis_index("dp"), lax.axis_index("mp")
-    mine = jnp.int32(0)
-    for b in range(16):
-        mine += jnp.where(slots_ref[mp, b] == dp, b, 0)
+    for copy in loads[4:]:
+        copy.wait()
+    mine = held(dp)
     hits = jnp.int32(0)
     for j in range(4):
-        hits += jnp.where(refresh_ref[mp, j] == mine, 1, 0)
-
-    @pl.when(hits > 0)
-    def _():
-        grad = grad_ref[...]
-        left = lax.dot_general(grad, grad, (((1,), (1,)), ((), ())), preferred_element_type=jnp.float32)
-        nl_ref[...] = inverse_root(0.9 * lf_ref[...] + left)
-        right = lax.dot_general(grad, grad, (((0,), (0,)), ((), ())), preferred_element_type=jnp.float32)
-        nr_ref[...] = inverse_root(0.9 * rf_ref[...] + right)
-
-    @pl.when(hits == 0)
-    def _():
-        nl_ref[...] = lr_ref[...]
-        nr_ref[...] = rr_ref[...]
-
-    grad = grad_ref[...]
+        hits += jnp.where(refresh_ref[j, mp] == mine, 1, 0)
+    chosen = jnp.broadcast_to(hits > 0, (SIDE, SIDE))
+    grad = tile[...]
+    left = lax.dot_general(grad, grad, (((1,), (1,)), ((), ())), preferred_element_type=jnp.float32)
+    right = lax.dot_general(grad, grad, (((0,), (0,)), ((), ())), preferred_element_type=jnp.float32)
+    lroot, rroot = inverse_roots((0.9 * lf_ref[...] + left, 0.9 * rf_ref[...] + right))
+    nl_ref[...] = jnp.where(chosen, lroot, lr_ref[...])
+    nr_ref[...] = jnp.where(chosen, rroot, rr_ref[...])
     mixed = jnp.dot(nl_ref[...], grad, preferred_element_type=jnp.float32).astype(jnp.bfloat16)
     precond = jnp.dot(mixed, nr_ref[...], preferred_element_type=jnp.float32)
     wide = grad.astype(jnp.float32)
     ratio = jnp.sqrt((jnp.sum(wide * wide) + 1e-06) / (jnp.sum(precond * precond) + 1e-06))
-    dir_ref[...] = (precond * ratio).astype(jnp.bfloat16)
-
-
-def slot_step(block_slot, refresh_list, gradient, left_factor, right_factor, left_root, right_root):
-    vmem = pl.BlockSpec(memory_space=pltpu.VMEM)
-    smem = pl.BlockSpec(memory_space=pltpu.SMEM)
-    tile = jax.ShapeDtypeStruct((SIDE, SIDE), jnp.bfloat16)
-    return pl.pallas_call(
-        slot_kernel,
-        name="slot_step",
-        out_shape=(tile, tile, tile),
-        in_specs=[smem, smem] + [vmem] * 5,
-        out_specs=(vmem, vmem, vmem),
-        compiler_params=pltpu.CompilerParams(vmem_limit_bytes=VMEM_LIMIT),
-        cost_estimate=pl.CostEstimate(flops=2 * 512**3 * 20, bytes_accessed=5 << 20, transcendentals=0),
-    )(block_slot, refresh_list, gradient, left_factor, right_factor, left_root, right_root)
-
-
-def spread_kernel(
-    tile_ref, every, z_s, z_r, zb_s, zb_r, y_s, y_r, yb_s, yb_r, local_s
-):
-    z, h, l, x, k = place()
-    dp, mp = lax.axis_index("dp"), lax.axis_index("mp")
-    ends = ((2 * ((z + 1) % NZ) + h, mp), (2 * ((z + NZ - 1) % NZ) + h, mp))
+    every[dp] = (precond * ratio).astype(jnp.bfloat16)
+
+    ends = ((2 * up + h, mp), (2 * down + h, mp))
     partner = (2 * z + 1 - h, mp)
-    barrier = pltpu.get_barrier_semaphore()
-    for target in (*ends, partner):
-        pl.semaphore_signal(barrier, inc=1, device_id=target, device_id_type=MESH)
-    own = pltpu.make_async_copy(tile_ref, every.at[dp], local_s)
-    own.start()
-    pl.semaphore_wait(barrier, 3)
-
-    pending = []
-
-    def send(src, dst, ssem, rsem, target):
-        copy = pltpu.make_async_remote_copy(
-            src_ref=src, dst_ref=dst, send_sem=ssem, recv_sem=rsem, device_id=target, device_id_type=MESH
-        )
-        copy.start()
-        pending.append(copy)
 
     def arrived(view, sem):
         pltpu.make_async_copy(view, view, sem).wait()
@@ -355,6 +281,9 @@
             return pl.ds(0, A_ROWS)
         return pl.ds(direction * HALF, HALF)
 
+    def post(src, dst, ssem, rsem, target):
+        pending.append(send(src, dst, ssem, rsem, target))
+
     def a_view(slot, rows):
         return every.at[slot, rows, :]
 
@@ -364,24 +293,23 @@
     def z_a(direction, step):
         rows = a_rows(direction, step)
         dst = a_view(2 * source(direction, step) + h, rows)
-        src = tile_ref.at[rows, :] if step == 0 else dst
-        send(src, dst, z_s.at[direction, step], z_r.at[direction, step], ends[direction])
+        src = dst
+        post(src, dst, z_s.at[direction, step], z_r.at[direction, step], ends[direction])
 
     def z_b(direction, step, u):
         dst = b_view(2 * source(direction, step) + u)
         src = dst
-        send(src, dst, zb_s.at[direction, step, u], zb_r.at[direction, step, u], ends[direction])
-
-    def y_a(index, slot, rows, src=None):
+        post(src, dst, zb_s.at[direction, step, u], zb_r.at[direction, step, u], ends[direction])
+
+    def y_a(index, slot, rows):
         dst = a_view(slot, rows)
-        send(dst if src is None else src, dst, y_s.at[index], y_r.at[index], partner)
+        post(dst, dst, y_s.at[index], y_r.at[index], partner)
 
     full = pl.ds(0, A_ROWS)
     z_a(0, 0)
     z_a(1, 0)
-    send(tile_ref.at[pl.ds(A_ROWS, SIDE - A_ROWS), :], b_view(dp), yb_s, yb_r, partner)
-    y_a(0, dp, full, tile_ref.at[full, :])
-    own.wait()
+    post(b_view(dp), b_view(dp), yb_s, yb_r, partner)
+    y_a(0, dp, full)
     z_b(0, 0, h)
     z_b(1, 0, h)
     arrived(b_view(2 * z + 1 - h), yb_r)
@@ -417,43 +345,94 @@
             arrived(a_view(2 * source(direction, step) + other, full), y_r.at[1 + 3 * direction + step - 1])
     for direction in (0, 1):
         arrived(a_view(2 * source(direction, 4) + other, a_rows(direction, 3)), y_r.at[7 + direction])
+
     for copy in pending:
         copy.wait_send()
-
-
-def spread(tile):
+    for j in range(4):
+        here = jnp.logical_and(4 * k + j == z, z % 2 == k)
+        src = flipped.at[j * FEAT : (j + 1) * FEAT, :]
+
+        @pl.when(jnp.logical_not(here))
+        def _():
+            pltpu.make_async_copy(src, src, turn_s.at[j]).wait()
+
+
+def step(block_slot, refresh_list, activations, out_grad, left_factor, right_factor, left_root, right_root):
     dma = pltpu.SemaphoreType.DMA
+    vmem = pl.BlockSpec(memory_space=pltpu.VMEM)
+    tile = jax.ShapeDtypeStruct((SIDE, SIDE), jnp.bfloat16)
     return pl.pallas_call(
-        spread_kernel,
-        name="spread",
-        out_shape=jax.ShapeDtypeStruct((16, SIDE, SIDE), jnp.bfloat16),
-        in_specs=[pl.BlockSpec(memory_space=pl.ANY)],
-        out_specs=pl.BlockSpec(memory_space=pl.ANY),
+        step_kernel,
+        name="step",
+        out_shape=(jax.ShapeDtypeStruct((16, SIDE, SIDE), jnp.bfloat16), tile, tile),
+        in_specs=[pl.BlockSpec(memory_space=pltpu.HBM)] * 8,
+        out_specs=(vmem, vmem, vmem),
         scratch_shapes=[
-            dma((2, 4)), dma((2, 4)), dma((2, 4, 2)), dma((2, 4, 2)), dma((9,)), dma((9,)), dma, dma, dma,
+            pltpu.SMEM((16, 16), jnp.int32),
+            pltpu.SMEM((4, 16), jnp.int32),
+            pltpu.VMEM((128, 256), jnp.bfloat16),
+            pltpu.VMEM((128, 1024), jnp.bfloat16),
+            pltpu.VMEM((SIDE, SIDE), jnp.float32),
+            pltpu.VMEM((SIDE, SIDE), jnp.float32),
+            pltpu.VMEM((SIDE, SIDE), jnp.bfloat16),
+            pltpu.VMEM((SIDE, SIDE), jnp.bfloat16),
+            dma((8,)),
+            pltpu.VMEM((NZ, 256, SIDE), jnp.bfloat16),
+            pltpu.VMEM((4, 2, 8, FEAT, 256), jnp.bfloat16),
+            pltpu.VMEM((256, 128), jnp.bfloat16),
+            pltpu.VMEM((8 * FEAT, SIDE), jnp.float32),
+            pltpu.VMEM((16, FEAT, 256), jnp.bfloat16),
+            pltpu.VMEM((16, FEAT, 256), jnp.bfloat16),
+            pltpu.VMEM((SIDE, SIDE), jnp.bfloat16),
+            dma((2,)), dma((2,)), dma((2, 4, 2)), dma((2, 4, 2)), dma((4,)), dma((NZ,)), dma((16,)), dma((16,)),
+            dma((8,)), dma((8,)), dma((16,)), dma((16,)), dma,
+            dma((2, 4)), dma((2, 4)), dma((2, 4, 2)), dma((2, 4, 2)), dma((9,)), dma((9,)), dma, dma,
         ],
-        compiler_params=pltpu.CompilerParams(collective_id=2, has_side_effects=True),
-        cost_estimate=pl.CostEstimate(flops=0, bytes_accessed=16 << 20, transcendentals=0),
-    )(tile)
-
-
-def arrange_kernel(slots_ref, every, out_ref):
-    out_ref[...] = every[0]
-
-
-def arrange(slot_row, every):
+        compiler_params=pltpu.CompilerParams(collective_id=1, has_side_effects=True, vmem_limit_bytes=VMEM_LIMIT),
+        cost_estimate=pl.CostEstimate(flops=2 * 512**3 * 24, bytes_accessed=20 << 20, transcendentals=0),
+    )(*(
+        pltpu.with_memory_space_constraint(x, pltpu.HBM)
+        for x in (block_slot, refresh_list.T, activations, out_grad, left_factor, right_factor, left_root, right_root)
+    ))
+
+
+def arrange_kernel(slots_hbm, every, left, right, out_hbm, nl_hbm, nr_hbm, slots_ref, sem):
+    mp = lax.axis_index("mp")
+    load = pltpu.make_async_copy(slots_hbm, slots_ref, sem.at[16])
+    load.start()
+    copies = [
+        pltpu.make_async_copy(left, nl_hbm, sem.at[17]),
+        pltpu.make_async_copy(right, nr_hbm, sem.at[18]),
+    ]
+    for copy in copies:
+        copy.start()
+    load.wait()
+    for b in range(16):
+        copy = pltpu.make_async_copy(
+            every.at[slots_ref[mp, b]],
+            out_hbm.at[pl.ds((b // 2) * SIDE, SIDE), pl.ds((b % 2) * SIDE, SIDE)],
+            sem.at[b],
+        )
+        copy.start()
+        copies.append(copy)
+    for copy in copies:
+        copy.wait()
+
+
+def arrange(block_slot, every, left, right):
+    hbm = pl.BlockSpec(memory_space=pltpu.HBM)
+    vmem = pl.BlockSpec(memory_space=pltpu.VMEM)
+    tile = jax.ShapeDtypeStruct((SIDE, SIDE), jnp.bfloat16)
     return pl.pallas_call(
         arrange_kernel,
         name="arrange",
-        grid_spec=pltpu.PrefetchScalarGridSpec(
-            num_scalar_prefetch=1,
-            grid=(16,),
-            in_specs=[pl.BlockSpec((1, SIDE, SIDE), lambda b, slots: (slots[b], 0, 0))],
-            out_specs=pl.BlockSpec((SIDE, SIDE), lambda b, slots: (b // 2, b % 2)),
-        ),
-        out_shape=jax.ShapeDtypeStruct((8 * SIDE, 2 * SIDE), jnp.bfloat16),
+        in_specs=[hbm, vmem, vmem, vmem],
+        out_specs=(hbm, hbm, hbm),
+        out_shape=(jax.ShapeDtypeStruct((8 * SIDE, 2 * SIDE), jnp.bfloat16), tile, tile),
+        scratch_shapes=[pltpu.SMEM((16, 16), jnp.int32), pltpu.SemaphoreType.DMA((19,))],
+        compiler_params=pltpu.CompilerParams(vmem_limit_bytes=VMEM_LIMIT),
         cost_estimate=pl.CostEstimate(flops=0, bytes_accessed=16 << 20, transcendentals=0),
-    )(slot_row, every)
+    )(pltpu.with_memory_space_constraint(block_slot, pltpu.HBM), every, left, right)
 
 
 def body(
@@ -466,13 +445,11 @@
     left_root,
     right_root,
 ):
-    slot_row = lax.dynamic_index_in_dim(block_slot, lax.axis_index("mp"), 0, keepdims=False)
-    gradient = owned_gradient(block_slot, activations, out_grad)
-    tile, new_left, new_right = slot_step(
-        block_slot, refresh_list, gradient,
+    every, new_left, new_right = step(
+        block_slot, refresh_list, activations, out_grad,
         left_factor[0, 0], right_factor[0, 0], left_root[0, 0], right_root[0, 0],
     )
-    direction = arrange(slot_row, spread(tile))
+    direction, new_left, new_right = arrange(block_slot, every, new_left, new_right)
     return (direction, new_left[None, None], new_right[None, None])
 
 

time: 157 us -> 127 us (0.81)
  the two profiles are of different devices: /device:TPU:14 before, /device:TPU:10 now
where the time goes in v2:
time: 127 us; the launch traced here: 125 us
  Pallas kernels  125 us (98%)
    pallas_call x1, Pallas kernels, step(): pl.pallas_call(step_kernel, name='step', out_shape=(jax.ShapeDtypeStruct(...  120 us
    pallas_call x1, Pallas kernels, arrange(): pl.pallas_call(arrange_kernel, name='arrange', in_specs=[hbm, vmem, vmem,...  4.21 us

profile of v2, /device:TPU:10, one launch (start us, length us, event | category | flops | bytes accessed | tf_op | source)
XLA Modules:
  0.0 125.1 jit_solution(8246848362419667626)
XLA Ops:
  0.6 120.3 %step.1 = (bf16[16,512,512]{2,1,0:T(8,128)(2,1)S(1)}, bf16[512,512]{1,0:T(8,128)(2,1)S(1)}, bf16[512,512]{1,0:T(8,128)(2,1)S(1)}) custom-call(s32[16,16]{1,0:T(8,128)} %slots_hbm.3, s32[4,16]{1,0:T(4,128)} %bitcast.13, bf16[128,256]{1,0:T(8,128)(2,1)} %act_hbm.1, bf16[128,1024]{1,0:T(8,128)(2,1)} %out_hbm.1, f32[512,512]{1,0:T(8,128)} %bitcast.7, ...), custom_call_target="tpu_custom_call" | custom-call | flops 6442450944 | bytes 20971520 | tf_op jit(solution)/shard_map/step/pallas_call | solution.py:364
  120.9 4.2 %arrange.1 = (bf16[4096,1024]{1,0:T(8,128)(2,1)}, bf16[512,512]{1,0:T(8,128)(2,1)}, bf16[512,512]{1,0:T(8,128)(2,1)}) custom-call(s32[16,16]{1,0:T(8,128)} %slots_hbm.3, bf16[16,512,512]{2,1,0:T(8,128)(2,1)S(1)} %get-tuple-element.9.every, bf16[512,512]{1,0:T(8,128)(2,1)S(1)} %get-tuple-element.10.left, bf16[512,512]{1,0:T(8,128)(2,1)S(1)} %get-tuple-element.11.right), custom_call_target="tpu_custom_call" | custom-call | bytes 16777216 | tf_op jit(solution)/shard_map/arrange/pallas_call | solution.py:426

commit v3 on v2

--- a/solution.py
+++ b/solution.py
@@ -49,14 +49,13 @@
 
 def step_kernel(
     slots_hbm, refresh_hbm, act_hbm, out_hbm, lf_hbm, rf_hbm, lr_hbm, rr_hbm, every, nl_ref, nr_ref,
-    slots_ref, refresh_ref, act_ref, out_ref, lf_ref, rf_ref, lr_ref, rr_ref, load_s, cot, act, flipped, total, pieces, outgoing, tile,
+    slots_ref, refresh_ref, act_ref, out_ref, lf_ref, rf_ref, lr_ref, rr_ref, load_s, cot, act, flipped, total, table, outgoing, tile,
     swap_s, swap_r, ring_s, ring_r, turn_s, turn_r, plane_s, plane_r,
     pass_s, pass_r, give_s, give_r, local_s, z_s, z_r, zb_s, zb_r, y_s, y_r, yb_s, yb_r,
 ):
     z, h, l, x, k = place()
     dp, mp = lax.axis_index("dp"), lax.axis_index("mp")
     y = 2 * h + l
-    r = 4 * l + x
     up, down = (z + 1) % NZ, (z + NZ - 1) % NZ
 
     loads = [
@@ -72,18 +71,23 @@
         copy.start()
     barrier = pltpu.get_barrier_semaphore()
 
+    def x_peer(step):
+        return device(z, h, l, (x + step) % NX, k)
+
+    def y_peer(step):
+        there = (y + step) % NY
+        return device(z, there // 2, there % 2, x, k)
+
     def greet(target):
         pl.semaphore_signal(barrier, inc=1, device_id=target, device_id_type=MESH)
 
-    for step in range(1, 16):
-        greet(((dp + step) % 16, mp))
-    for dy in range(NY):
-        for dx in range(NX):
-            if (dy, dx) != (0, 0):
-                ty, tx = (y + dy) % NY, (x + dx) % NX
-                greet(device(z, ty // 2, ty % 2, tx, k))
+    for step in range(1, NZ):
+        greet(device((z + step) % NZ, h, l, x, k))
     for step in range(NZ):
         greet(device((z + step) % NZ, h, l, x, 1 - k))
+    for step in range(1, 4):
+        greet(x_peer(step))
+        greet(y_peer(step))
 
     for copy in loads[:4]:
         copy.wait()
@@ -91,8 +95,7 @@
         cot[z, pl.ds(h * 128, 128), c * 256 : c * 256 + 256] = out_ref[
             :, pl.ds(pl.multiple_of(c * 512 + 256 * h, 256), 256)
         ]
-    flipped[...] = act_ref[...].astype(jnp.float32).T.astype(jnp.bfloat16)
-    pl.semaphore_wait(barrier, 38)
+    pl.semaphore_wait(barrier, 21)
 
     def send(src, dst, ssem, rsem, target):
         copy = pltpu.make_async_remote_copy(
@@ -102,22 +105,6 @@
         return copy
 
     pending = []
-
-    def turn_view(source):
-        return act.at[source // 2, source % 2, r, :, pl.ds(pl.multiple_of(h * 128, 128), 128)]
-
-    for j in range(4):
-        target = 4 * k + j
-        here = jnp.logical_and(target == z, z % 2 == k)
-        src = flipped.at[j * FEAT : (j + 1) * FEAT, :]
-
-        @pl.when(jnp.logical_not(here))
-        def _():
-            send(src, turn_view(z), turn_s.at[j], turn_r.at[z], device(target, h, l, x, z % 2))
-
-        @pl.when(here)
-        def _():
-            pltpu.make_async_copy(src, turn_view(z), turn_r.at[z]).start()
 
     for c in range(2):
         pending.append(
@@ -150,22 +137,24 @@
     ring(0, 0, h)
     ring(1, 0, h)
 
-    for i in range(4):
-        source = 2 * i + k
-        view = turn_view(source)
-        pltpu.make_async_copy(view, view, turn_r.at[source]).wait()
-
-    def plane_view(row, half):
-        return act.at[:, k, row, :, pl.ds(pl.multiple_of(half * 128, 128), 128)]
-
-    for dy in range(NY):
-        for dx in range(NX):
-            if (dy, dx) != (0, 0):
-                ty, tx = (y + dy) % NY, (x + dx) % NX
-                view = plane_view(r, h)
-                pending.append(
-                    send(view, view, plane_s.at[4 * dy + dx], plane_r.at[4 * dy + dx], device(z, ty // 2, ty % 2, tx, k))
-                )
+
+    flipped[...] = act_ref[...].astype(jnp.float32).T.astype(jnp.bfloat16)
+
+    def turn_view(source):
+        return act.at[source // 2, source % 2, l, x, :, pl.ds(pl.multiple_of(h * 128, 128), 128)]
+
+    for j in range(4):
+        target = 4 * k + j
+        here = jnp.logical_and(target == z, z % 2 == k)
+        src = flipped.at[j * FEAT : (j + 1) * FEAT, :]
+
+        @pl.when(jnp.logical_not(here))
+        def _():
+            send(src, turn_view(z), turn_s.at[j], turn_r.at[z], device(target, h, l, x, z % 2))
+
+        @pl.when(here)
+        def _():
+            pltpu.make_async_copy(src, turn_view(z), turn_r.at[z]).start()
 
     for c in range(2):
         view = cot.at[z, pl.ds(pl.multiple_of((1 - h) * 128, 128), 128), pl.ds(c * 256, 256)]
@@ -173,21 +162,66 @@
     ring(0, 0, 1 - h)
     ring(1, 0, 1 - h)
 
-    for step in (1, 2):
+    for i in range(4):
+        source = 2 * i + k
+        view = turn_view(source)
+        pltpu.make_async_copy(view, view, turn_r.at[source]).wait()
+
+    def tokens(half):
+        return pl.ds(pl.multiple_of(half * 128, 128), 128)
+
+    def first_view(part, col, row):
+        return act.at[2 * part : 2 * part + 2, k, row % 2, col, :, tokens(row // 2)]
+
+    def second_view(part, index):
+        if part == 0:
+            return act.at[0:2, k, index % 2, :, :, tokens(index // 2)]
+        return act.at[2:4, k, :, index]
+
+    def peer(axis, step):
+        return x_peer(step) if axis == 0 else y_peer(step)
+
+    def back(axis, step):
+        return (x + NX - step) % NX if axis == 0 else (y + NY - step) % NY
+
+    for step in (1, 2, 3):
+        for part in (0, 1):
+            view = first_view(part, x, y)
+            pending.append(send(view, view, plane_s.at[0, part, step], plane_r.at[0, part, step], peer(part, step)))
+
+    def advance(step):
         for u in (h, 1 - h):
             for direction in (0, 1):
                 ring_wait(direction, step, u)
                 ring(direction, step, u)
 
-    for dy in range(NY):
-        for dx in range(NX):
-            if (dy, dx) != (0, 0):
-                sy, sx = (y + NY - dy) % NY, (x + NX - dx) % NX
-                view = plane_view(4 * (sy % 2) + sx, sy // 2)
-                pltpu.make_async_copy(view, view, plane_r.at[4 * dy + dx]).wait()
-    for row in range(8):
-        view = act.at[:, k, row]
-        pending.append(send(view, view, pass_s.at[row], pass_r.at[row], device(z, h, l, x, 1 - k)))
+    advance(1)
+    for part in (0, 1):
+        for step in (1, 2, 3):
+            view = first_view(0, back(0, step), y) if part == 0 else first_view(1, x, back(1, step))
+            pltpu.make_async_copy(view, view, plane_r.at[0, part, step]).wait()
+        view = second_view(part, y if part == 0 else x)
+        for step in (1, 2, 3):
+            pending.append(
+                send(view, view, plane_s.at[1, part, step], plane_r.at[1, part, step], peer(1 - part, step))
+            )
+    advance(2)
+
+    for part in (0, 1):
+        for step in (1, 2, 3):
+            view = second_view(part, back(1 - part, step))
+            pltpu.make_async_copy(view, view, plane_r.at[1, part, step]).wait()
+        view = act.at[2 * part : 2 * part + 2, k]
+        pending.append(send(view, view, pass_s.at[part], pass_r.at[part], device(z, h, l, x, 1 - k)))
+
+    def held(slot):
+        found = jnp.int32(0)
+        for b in range(16):
+            found = jnp.maximum(found, jnp.where(slots_ref[mp, b] == slot, b, 0))
+        return found
+
+    for slot in range(16):
+        table[slot] = held(slot)
 
     for u in (h, 1 - h):
         for direction in (0, 1):
@@ -195,48 +229,46 @@
     ring(0, 3, 0)
     ring(1, 3, 1)
 
-    for row in range(8):
-        view = act.at[:, 1 - k, row]
-        pltpu.make_async_copy(view, view, pass_r.at[row]).wait()
+    for part in (0, 1):
+        view = act.at[2 * part : 2 * part + 2, 1 - k]
+        pltpu.make_async_copy(view, view, pass_r.at[part]).wait()
 
     def product(source):
         return jnp.dot(
             act[source // 2, source % 2].reshape(8 * FEAT, 256), cot[source], preferred_element_type=jnp.float32
         )
 
-    total[...] = product(z)
+    def add(value):
+        for c in range(2):
+            total[:, c] += value[:, c * 256 : (c + 1) * 256].reshape(8, FEAT, 256)
+
+    total[...] = jnp.zeros_like(total)
+    add(product(z))
 
     @pl.loop(1, 4)
     def _(step):
-        total[...] += product((z + step) % NZ)
-        total[...] += product((z + NZ - step) % NZ)
+        add(product((z + step) % NZ) + product((z + NZ - step) % NZ))
 
     ring_wait(0, 4, 0)
     ring_wait(1, 4, 1)
-    total[...] += product((z + 4) % NZ)
-
-    for row in range(8):
-        for c in range(2):
-            pieces[2 * row + c] = total[row * FEAT : (row + 1) * FEAT, c * 256 : (c + 1) * 256].astype(jnp.bfloat16)
+    add(product((z + 4) % NZ))
+
+    def piece(slot):
+        block = table[slot]
+        return total[block // 2, block % 2].astype(jnp.bfloat16)
 
     def spot(slot):
         return tile.at[
             pl.ds(pl.multiple_of((slot // 2) * FEAT, FEAT), FEAT), pl.ds(pl.multiple_of((slot % 2) * 256, 256), 256)
         ]
 
-    def held(slot):
-        found = jnp.int32(0)
-        for b in range(16):
-            found = jnp.maximum(found, jnp.where(slots_ref[mp, b] == slot, b, 0))
-        return found
-
     @pl.loop(1, 16)
     def _(step):
         slot = (dp + step) % 16
-        outgoing[slot] = pieces[held(slot)]
+        outgoing[slot] = piece(slot)
         send(outgoing.at[slot], spot(dp), give_s.at[slot], give_r.at[dp], (slot, mp))
 
-    outgoing[dp] = pieces[held(dp)]
+    outgoing[dp] = piece(dp)
     own = pltpu.make_async_copy(outgoing.at[dp], spot(dp), local_s)
     own.start()
     own.wait()
@@ -246,11 +278,10 @@
         slot = (dp + step) % 16
         view = spot(slot)
         pltpu.make_async_copy(view, view, give_r.at[slot]).wait()
-        pltpu.make_async_copy(outgoing.at[slot], outgoing.at[slot], give_s.at[slot]).wait()
 
     for copy in loads[4:]:
         copy.wait()
-    mine = held(dp)
+    mine = table[dp]
     hits = jnp.int32(0)
     for j in range(4):
         hits += jnp.where(refresh_ref[j, mp] == mine, 1, 0)
@@ -348,6 +379,12 @@
 
     for copy in pending:
         copy.wait_send()
+
+    @pl.loop(1, 16)
+    def _(step):
+        slot = (dp + step) % 16
+        pltpu.make_async_copy(outgoing.at[slot], outgoing.at[slot], give_s.at[slot]).wait()
+
     for j in range(4):
         here = jnp.logical_and(4 * k + j == z, z % 2 == k)
         src = flipped.at[j * FEAT : (j + 1) * FEAT, :]
@@ -378,14 +415,14 @@
             pltpu.VMEM((SIDE, SIDE), jnp.bfloat16),
             dma((8,)),
             pltpu.VMEM((NZ, 256, SIDE), jnp.bfloat16),
-            pltpu.VMEM((4, 2, 8, FEAT, 256), jnp.bfloat16),
+            pltpu.VMEM((4, 2, 2, NX, FEAT, 256), jnp.bfloat16),
             pltpu.VMEM((256, 128), jnp.bfloat16),
-            pltpu.VMEM((8 * FEAT, SIDE), jnp.float32),
-            pltpu.VMEM((16, FEAT, 256), jnp.bfloat16),
+            pltpu.VMEM((8, 2, FEAT, 256), jnp.float32),
+            pltpu.SMEM((16,), jnp.int32),
             pltpu.VMEM((16, FEAT, 256), jnp.bfloat16),
             pltpu.VMEM((SIDE, SIDE), jnp.bfloat16),
-            dma((2,)), dma((2,)), dma((2, 4, 2)), dma((2, 4, 2)), dma((4,)), dma((NZ,)), dma((16,)), dma((16,)),
-            dma((8,)), dma((8,)), dma((16,)), dma((16,)), dma,
+            dma((2,)), dma((2,)), dma((2, 4, 2)), dma((2, 4, 2)), dma((4,)), dma((NZ,)), dma((2, 2, 4)), dma((2, 2, 4)),
+            dma((2,)), dma((2,)), dma((16,)), dma((16,)), dma,
             dma((2, 4)), dma((2, 4)), dma((2, 4, 2)), dma((2, 4, 2)), dma((9,)), dma((9,)), dma, dma,
         ],
         compiler_params=pltpu.CompilerParams(collective_id=1, has_side_effects=True, vmem_limit_bytes=VMEM_LIMIT),

time: 127 us -> 124 us (0.976)
  Pallas kernels: 125 us -> 122 us
    pallas_call x1, Pallas kernels: 120 us -> 118 us  [step(): pl.pallas_call(step_kernel, name='step', out_shape=(jax.ShapeDtypeStruct(...]
where the time goes in v3:
time: 124 us; the launch traced here: 123 us
  Pallas kernels  122 us (98%)
    pallas_call x1, Pallas kernels, step(): pl.pallas_call(step_kernel, name='step', out_shape=(jax.ShapeDtypeStruct(...  118 us
    pallas_call x1, Pallas kernels, arrange(): pl.pallas_call(arrange_kernel, name='arrange', in_specs=[hbm, vmem, vmem,...  4.21 us

profile of v3, /device:TPU:10, one launch (start us, length us, event | category | flops | bytes accessed | tf_op | source)
XLA Modules:
  0.0 122.7 jit_solution(16881566147745961089)
XLA Ops:
  0.6 117.9 %step.1 = (bf16[16,512,512]{2,1,0:T(8,128)(2,1)S(1)}, bf16[512,512]{1,0:T(8,128)(2,1)S(1)}, bf16[512,512]{1,0:T(8,128)(2,1)S(1)}) custom-call(s32[16,16]{1,0:T(8,128)} %slots_hbm.3, s32[4,16]{1,0:T(4,128)} %bitcast.13, bf16[128,256]{1,0:T(8,128)(2,1)} %act_hbm.1, bf16[128,1024]{1,0:T(8,128)(2,1)} %out_hbm.1, f32[512,512]{1,0:T(8,128)} %bitcast.7, ...), custom_call_target="tpu_custom_call" | custom-call | flops 6442450944 | bytes 20971520 | tf_op jit(solution)/shard_map/step/pallas_call | solution.py:401
  118.5 4.2 %arrange.1 = (bf16[4096,1024]{1,0:T(8,128)(2,1)}, bf16[512,512]{1,0:T(8,128)(2,1)}, bf16[512,512]{1,0:T(8,128)(2,1)}) custom-call(s32[16,16]{1,0:T(8,128)} %slots_hbm.3, bf16[16,512,512]{2,1,0:T(8,128)(2,1)S(1)} %get-tuple-element.9.every, bf16[512,512]{1,0:T(8,128)(2,1)S(1)} %get-tuple-element.10.left, bf16[512,512]{1,0:T(8,128)(2,1)S(1)} %get-tuple-element.11.right), custom_call_target="tpu_custom_call" | custom-call | bytes 16777216 | tf_op jit(solution)/shard_map/arrange/pallas_call | solution.py:463

commit v4 on v3

--- a/solution.py
+++ b/solution.py
@@ -23,27 +23,34 @@
     return (2 * z + h, 8 * l + 2 * x + k)
 
 
-def matmul(left, right):
-    return jnp.dot(left.astype(jnp.bfloat16), right.astype(jnp.bfloat16), preferred_element_type=jnp.float32)
-
-
 def inverse_roots(statistics):
     shape = statistics[0].shape
     rows = lax.broadcasted_iota(jnp.int32, shape, 0)
     cols = lax.broadcasted_iota(jnp.int32, shape, 1)
     identity = jnp.where(rows == cols, 1.0, 0.0).astype(jnp.float32)
+
+    def dot(left, right):
+        return jnp.dot(left, right, preferred_element_type=jnp.float32)
+
+    def half(values):
+        return [v.astype(jnp.bfloat16) for v in values]
+
+    def next_dev(dev, narrow):
+        square = half([dot(n, n) + (1.5625 * identity - 2.5 * e) for e, n in zip(dev, narrow)])
+        fourth = half([dot(f, f) for f in square])
+        return [dot(f, n) for f, n in zip(fourth, narrow)]
+
     scaling = [2.5 / jnp.sqrt(jnp.sum(a * a)) for a in statistics]
-    powered = [a * c for a, c in zip(statistics, scaling)]
-    parts = []
-    for _ in range(2):
-        dev = [0.25 * m for m in powered]
-        parts.append(dev)
-        square = [1.5625 * identity - 2.5 * e + matmul(e, e) for e in dev]
-        fourth = [matmul(f, f) for f in square]
-        powered = [matmul(f, m) for f, m in zip(fourth, powered)]
-    third = [0.25 * m for m in powered]
-    pair = [1.25 * (e + f) - matmul(e, f) for e, f in zip(*parts)]
-    result = [1.953125 * identity - 1.25 * p - 1.5625 * e + matmul(p, e) for p, e in zip(pair, third)]
+    first = [a * (0.25 * c) for a, c in zip(statistics, scaling)]
+    first_n = half(first)
+    second = next_dev(first, first_n)
+    second_n = half(second)
+    pair = [1.25 * (e + f) - dot(m, n) for e, f, m, n in zip(first, second, first_n, second_n)]
+    third = next_dev(second, second_n)
+    result = [
+        1.953125 * identity - 1.25 * p - 1.5625 * e + dot(m, n)
+        for p, e, m, n in zip(pair, third, half(pair), half(third))
+    ]
     return [(x * jnp.sqrt(jnp.sqrt(c))).astype(jnp.bfloat16) for x, c in zip(result, scaling)]
 
 
@@ -81,21 +88,24 @@
     def greet(target):
         pl.semaphore_signal(barrier, inc=1, device_id=target, device_id_type=MESH)
 
-    for step in range(1, NZ):
-        greet(device((z + step) % NZ, h, l, x, k))
-    for step in range(NZ):
-        greet(device((z + step) % NZ, h, l, x, 1 - k))
+    greet(device(up, h, l, x, k))
+    greet(device(down, h, l, x, k))
     for step in range(1, 4):
         greet(x_peer(step))
         greet(y_peer(step))
-
-    for copy in loads[:4]:
-        copy.wait()
+    for i in range(4):
+        source = 2 * i + k
+
+        @pl.when(jnp.logical_not(jnp.logical_and(source == z, z // 4 == k)))
+        def _():
+            greet(device(source, h, l, x, z // 4))
+
+    loads[1].wait()
     for c in range(2):
         cot[z, pl.ds(h * 128, 128), c * 256 : c * 256 + 256] = out_ref[
             :, pl.ds(pl.multiple_of(c * 512 + 256 * h, 256), 256)
         ]
-    pl.semaphore_wait(barrier, 21)
+    pl.semaphore_wait(barrier, 12 - jnp.where(jnp.logical_and(z // 4 == k, z % 2 == k), 1, 0))
 
     def send(src, dst, ssem, rsem, target):
         copy = pltpu.make_async_remote_copy(
@@ -138,6 +148,7 @@
     ring(1, 0, h)
 
 
+    loads[0].wait()
     flipped[...] = act_ref[...].astype(jnp.float32).T.astype(jnp.bfloat16)
 
     def turn_view(source):
@@ -220,6 +231,8 @@
             found = jnp.maximum(found, jnp.where(slots_ref[mp, b] == slot, b, 0))
         return found
 
+    loads[2].wait()
+    loads[3].wait()
     for slot in range(16):
         table[slot] = held(slot)
 
@@ -262,11 +275,12 @@
             pl.ds(pl.multiple_of((slot // 2) * FEAT, FEAT), FEAT), pl.ds(pl.multiple_of((slot % 2) * 256, 256), 256)
         ]
 
-    @pl.loop(1, 16)
-    def _(step):
-        slot = (dp + step) % 16
-        outgoing[slot] = piece(slot)
-        send(outgoing.at[slot], spot(dp), give_s.at[slot], give_r.at[dp], (slot, mp))
+    for dz in (4, 3, 5, 2, 6, 1, 7, 0):
+        for dh in (0, 1):
+            if (dz, dh) != (0, 0):
+                slot = 2 * ((z + dz) % NZ) + (h + dh) % 2
+                outgoing[slot] = piece(slot)
+                send(outgoing.at[slot], spot(dp), give_s.at[slot], give_r.at[dp], (slot, mp))
 
     outgoing[dp] = piece(dp)
     own = pltpu.make_async_copy(outgoing.at[dp], spot(dp), local_s)

time: 124 us -> 124 us (level)
  no operation moved by 1% of the time
where the time goes in v4:
time: 124 us
  Pallas kernels  123 us (99%)
    pallas_call x1, Pallas kernels, step(): pl.pallas_call(step_kernel, name='step', out_shape=(jax.ShapeDtypeStruct(...  119 us
    pallas_call x1, Pallas kernels, arrange(): pl.pallas_call(arrange_kernel, name='arrange', in_specs=[hbm, vmem, vmem,...  4.21 us

profile of v4, /device:TPU:10, one launch (start us, length us, event | category | flops | bytes accessed | tf_op | source)
XLA Modules:
  0.0 123.7 jit_solution(2714708648057518179)
XLA Ops:
  0.6 118.9 %step.1 = (bf16[16,512,512]{2,1,0:T(8,128)(2,1)S(1)}, bf16[512,512]{1,0:T(8,128)(2,1)S(1)}, bf16[512,512]{1,0:T(8,128)(2,1)S(1)}) custom-call(s32[16,16]{1,0:T(8,128)} %slots_hbm.3, s32[4,16]{1,0:T(4,128)} %bitcast.13, bf16[128,256]{1,0:T(8,128)(2,1)} %act_hbm.1, bf16[128,1024]{1,0:T(8,128)(2,1)} %out_hbm.1, f32[512,512]{1,0:T(8,128)} %bitcast.7, ...), custom_call_target="tpu_custom_call" | custom-call | flops 6442450944 | bytes 20971520 | tf_op jit(solution)/shard_map/step/pallas_call | solution.py:415
  119.5 4.2 %arrange.1 = (bf16[4096,1024]{1,0:T(8,128)(2,1)}, bf16[512,512]{1,0:T(8,128)(2,1)}, bf16[512,512]{1,0:T(8,128)(2,1)}) custom-call(s32[16,16]{1,0:T(8,128)} %slots_hbm.3, bf16[16,512,512]{2,1,0:T(8,128)(2,1)S(1)} %get-tuple-element.9.every, bf16[512,512]{1,0:T(8,128)(2,1)S(1)} %get-tuple-element.10.left, bf16[512,512]{1,0:T(8,128)(2,1)S(1)} %get-tuple-element.11.right), custom_call_target="tpu_custom_call" | custom-call | bytes 16777216 | tf_op jit(solution)/shard_map/arrange/pallas_call | solution.py:477

commit v5 on v4

--- a/solution.py
+++ b/solution.py
@@ -32,25 +32,32 @@
     def dot(left, right):
         return jnp.dot(left, right, preferred_element_type=jnp.float32)
 
-    def half(values):
-        return [v.astype(jnp.bfloat16) for v in values]
-
-    def next_dev(dev, narrow):
-        square = half([dot(n, n) + (1.5625 * identity - 2.5 * e) for e, n in zip(dev, narrow)])
-        fourth = half([dot(f, f) for f in square])
-        return [dot(f, n) for f, n in zip(fourth, narrow)]
+    def parts(value, wide):
+        high = value.astype(jnp.bfloat16)
+        return (high, (value - high.astype(jnp.float32)).astype(jnp.bfloat16)) if wide else (high,)
+
+    def product(left, right):
+        total = dot(left[0], right[0])
+        if len(left) == 2:
+            total += dot(left[0], right[1]) + dot(left[1], right[0])
+        return total
+
+    def next_dev(dev, wide):
+        narrow = [parts(e, wide) for e in dev]
+        d = [2.5 * e - product(n, n) for e, n in zip(dev, narrow)]
+        d_n = [parts(x, wide) for x in d]
+        h = [parts(3.125 * x - product(n, n), wide) for x, n in zip(d, d_n)]
+        return [2.44140625 * e - product(x, n) for e, x, n in zip(dev, h, narrow)]
+
+    def plain(left, right):
+        return dot(left.astype(jnp.bfloat16), right.astype(jnp.bfloat16))
 
     scaling = [2.5 / jnp.sqrt(jnp.sum(a * a)) for a in statistics]
     first = [a * (0.25 * c) for a, c in zip(statistics, scaling)]
-    first_n = half(first)
-    second = next_dev(first, first_n)
-    second_n = half(second)
-    pair = [1.25 * (e + f) - dot(m, n) for e, f, m, n in zip(first, second, first_n, second_n)]
-    third = next_dev(second, second_n)
-    result = [
-        1.953125 * identity - 1.25 * p - 1.5625 * e + dot(m, n)
-        for p, e, m, n in zip(pair, third, half(pair), half(third))
-    ]
+    second = next_dev(first, True)
+    third = next_dev(second, False)
+    pair = [1.25 * (e + f) - plain(e, f) for e, f in zip(first, second)]
+    result = [1.953125 * identity - 1.25 * p - 1.5625 * e + plain(p, e) for p, e in zip(pair, third)]
     return [(x * jnp.sqrt(jnp.sqrt(c))).astype(jnp.bfloat16) for x, c in zip(result, scaling)]
 
 

time: 124 us -> 128 us (1.032)
  Pallas kernels: 123 us -> 127 us
    pallas_call x1, Pallas kernels: 119 us -> 123 us  [step(): pl.pallas_call(step_kernel, name='step', out_shape=(jax.ShapeDtypeStruct(...]
where the time goes in v5:
time: 128 us; the launch traced here: 127 us
  Pallas kernels  127 us (99%)
    pallas_call x1, Pallas kernels, step(): pl.pallas_call(step_kernel, name='step', out_shape=(jax.ShapeDtypeStruct(...  123 us
    pallas_call x1, Pallas kernels, arrange(): pl.pallas_call(arrange_kernel, name='arrange', in_specs=[hbm, vmem, vmem,...  4.21 us

profile of v5, /device:TPU:10, one launch (start us, length us, event | category | flops | bytes accessed | tf_op | source)
XLA Modules:
  0.0 127.4 jit_solution(2748654829797289817)
XLA Ops:
  0.6 122.6 %step.1 = (bf16[16,512,512]{2,1,0:T(8,128)(2,1)S(1)}, bf16[512,512]{1,0:T(8,128)(2,1)S(1)}, bf16[512,512]{1,0:T(8,128)(2,1)S(1)}) custom-call(s32[16,16]{1,0:T(8,128)} %slots_hbm.3, s32[4,16]{1,0:T(4,128)} %bitcast.13, bf16[128,256]{1,0:T(8,128)(2,1)} %act_hbm.1, bf16[128,1024]{1,0:T(8,128)(2,1)} %out_hbm.1, f32[512,512]{1,0:T(8,128)} %bitcast.7, ...), custom_call_target="tpu_custom_call" | custom-call | flops 6442450944 | bytes 20971520 | tf_op jit(solution)/shard_map/step/pallas_call | solution.py:422
  123.2 4.2 %arrange.1 = (bf16[4096,1024]{1,0:T(8,128)(2,1)}, bf16[512,512]{1,0:T(8,128)(2,1)}, bf16[512,512]{1,0:T(8,128)(2,1)}) custom-call(s32[16,16]{1,0:T(8,128)} %slots_hbm.3, bf16[16,512,512]{2,1,0:T(8,128)(2,1)S(1)} %get-tuple-element.9.every, bf16[512,512]{1,0:T(8,128)(2,1)S(1)} %get-tuple-element.10.left, bf16[512,512]{1,0:T(8,128)(2,1)S(1)} %get-tuple-element.11.right), custom_call_target="tpu_custom_call" | custom-call | bytes 16777216 | tf_op jit(solution)/shard_map/arrange/pallas_call | solution.py:484

commit v6 on v5

--- a/solution.py
+++ b/solution.py
@@ -81,8 +81,7 @@
             )
         )
     ]
-    for copy in loads:
-        copy.start()
+    loads[1].start()
     barrier = pltpu.get_barrier_semaphore()
 
     def x_peer(step):
@@ -94,18 +93,21 @@
 
     def greet(target):
         pl.semaphore_signal(barrier, inc=1, device_id=target, device_id_type=MESH)
+
+    for i in range(4):
+        source = 2 * i + k
+
+        @pl.when(jnp.logical_not(jnp.logical_and(source == z, z // 4 == k)))
+        def _():
+            greet(device(source, h, l, x, z // 4))
 
     greet(device(up, h, l, x, k))
     greet(device(down, h, l, x, k))
     for step in range(1, 4):
         greet(x_peer(step))
         greet(y_peer(step))
-    for i in range(4):
-        source = 2 * i + k
-
-        @pl.when(jnp.logical_not(jnp.logical_and(source == z, z // 4 == k)))
-        def _():
-            greet(device(source, h, l, x, z // 4))
+    for copy in (loads[0], *loads[2:]):
+        copy.start()
 
     loads[1].wait()
     for c in range(2):

time: 128 us -> 127 us (level)
  no operation moved by 1% of the time
where the time goes in v6:
time: 127 us
  Pallas kernels  126 us (99%)
    pallas_call x1, Pallas kernels, step(): pl.pallas_call(step_kernel, name='step', out_shape=(jax.ShapeDtypeStruct(...  122 us
    pallas_call x1, Pallas kernels, arrange(): pl.pallas_call(arrange_kernel, name='arrange', in_specs=[hbm, vmem, vmem,...  4.21 us

profile of v6, /device:TPU:10, one launch (start us, length us, event | category | flops | bytes accessed | tf_op | source)
XLA Modules:
  0.0 127.0 jit_solution(12795953008240672080)
XLA Ops:
  0.6 122.1 %step.1 = (bf16[16,512,512]{2,1,0:T(8,128)(2,1)S(1)}, bf16[512,512]{1,0:T(8,128)(2,1)S(1)}, bf16[512,512]{1,0:T(8,128)(2,1)S(1)}) custom-call(s32[16,16]{1,0:T(8,128)} %slots_hbm.3, s32[4,16]{1,0:T(4,128)} %bitcast.13, bf16[128,256]{1,0:T(8,128)(2,1)} %act_hbm.1, bf16[128,1024]{1,0:T(8,128)(2,1)} %out_hbm.1, f32[512,512]{1,0:T(8,128)} %bitcast.7, ...), custom_call_target="tpu_custom_call" | custom-call | flops 6442450944 | bytes 20971520 | tf_op jit(solution)/shard_map/step/pallas_call | solution.py:424
  122.8 4.2 %arrange.1 = (bf16[4096,1024]{1,0:T(8,128)(2,1)}, bf16[512,512]{1,0:T(8,128)(2,1)}, bf16[512,512]{1,0:T(8,128)(2,1)}) custom-call(s32[16,16]{1,0:T(8,128)} %slots_hbm.3, bf16[16,512,512]{2,1,0:T(8,128)(2,1)S(1)} %get-tuple-element.9.every, bf16[512,512]{1,0:T(8,128)(2,1)S(1)} %get-tuple-element.10.left, bf16[512,512]{1,0:T(8,128)(2,1)S(1)} %get-tuple-element.11.right), custom_call_target="tpu_custom_call" | custom-call | bytes 16777216 | tf_op jit(solution)/shard_map/arrange/pallas_call | solution.py:486
